TPU v7x, 32 devices: a whole 2x2x4 slice. The times are simulated.
32 devices in a mesh: seq: 8 (over y, x, core), tensor: 4 (over z).
Axes of the slice: x: 2, y: 2, z: 4, core: 2. Of those that a mesh axis runs over, the one named last changes fastest.
Arguments:
- tokens: bfloat16 [1024, 4096], P('seq'), may hold values from -8 to 8
- segment_ids: int32 [1024], replicated, may hold values from -1 to 14, as said below
- routes: int32 [1024, 2], P('seq'), may hold values from 0 to 7, all different within a row; in each aligned block of 128 rows (0 to 127, 128 to 255, ...) at most 64 rows name the same one
- owners: int32 [15], replicated, may hold values from 0 to 7
- gain_attn: float32 [4096], replicated, may hold values from 0.5 to 1.5
- w_query: bfloat16 [4096, 4096], P(None, 'tensor'), may hold values from -1 to 1
- w_kv: bfloat16 [4096, 2048], P(None, 'tensor'), may hold values from -1 to 1
- w_out: bfloat16 [4096, 4096], P('tensor'), may hold values from -0.09375 to 0.09375
- gain_moe: float32 [4096], replicated, may hold values from 0.5 to 1.5
- w_router: float32 [4096, 8], replicated, may hold values from -0.09375 to 0.09375
- w_gate: bfloat16 [4096, 65536], P(None, ('seq', 'tensor')), may hold values from -0.09375 to 0.09375
- w_up: bfloat16 [4096, 65536], P(None, ('seq', 'tensor')), may hold values from -0.09375 to 0.09375
- w_down: bfloat16 [65536, 4096], P(('seq', 'tensor')), may hold values from -0.0625 to 0.0625
Outputs:
- layer_out: bfloat16 [1024, 4096], P('seq', 'tensor')
- kv_cache: bfloat16 [8192, 2048], P('seq', 'tensor')
Inputs may be any that keep to these rules, and one draw needn't show every extreme that they name: `segment_ids`: tokens 0 to 575 form segment 0; segments 1 to 14 follow in order, each of 8 to 31 tokens; all later tokens are -1. `routes`: in each aligned block of 128 rows no expert is named by more than 64 rows; the two experts of a row differ.
All inputs are finite; a program needn't handle non-finite values.
Results may differ from a plain program's by a relative error of at most 0.014.
Values may be sent and summed in bfloat16 or wider, within the bound.
A program may use at most 128 MiB of HBM per device.

v0:
```python
import jax
import jax.numpy as jnp
from jax import lax
from jax.sharding import PartitionSpec as P

HEADS = 32
KV_HEADS = 8
HEAD_DIM = 128
EXPERTS = 8


EPS = 1e-05
THETA = 1000000.0
FLOOR = -1e30


def rms_norm(rows, gain):
    values = rows.astype(jnp.float32)
    scale = lax.rsqrt(jnp.mean(values * values, axis=-1, keepdims=True) + EPS)
    return (values * scale * gain).astype(jnp.bfloat16)


def rotate(values, position):
    half = values.shape[-1] // 2
    freqs = THETA ** (-(jnp.arange(half, dtype=jnp.float32) * 2.0) / values.shape[-1])
    angles = position.astype(jnp.float32)[:, None] * freqs[None, :]
    cosine = jnp.cos(angles)[:, None, :]
    sine = jnp.sin(angles)[:, None, :]
    first = values[..., :half]
    second = values[..., half:]
    return jnp.concatenate(
        [first * cosine - second * sine, second * cosine + first * sine], axis=-1
    )


def segment_layout(segment_ids, owners):
    short_count = owners.shape[0] - 1
    labels = jnp.where(segment_ids < 0, short_count + 1, segment_ids)
    onehot = labels[:, None] == jnp.arange(short_count + 2, dtype=jnp.int32)[None, :]
    counts = jnp.sum(onehot.astype(jnp.int32), axis=0)
    starts = jnp.cumsum(counts) - counts
    seg_start = jnp.sum(jnp.where(onehot, starts[None, :], 0), axis=1)
    owner_ext = jnp.concatenate([owners, jnp.full((1,), -1, jnp.int32)])
    owner_tok = jnp.sum(jnp.where(onehot, owner_ext[None, :], 0), axis=1)
    return (seg_start, owner_tok)


def owner_slots(owner_tok, owner_count):
    hits = (owner_tok[:, None] == jnp.arange(owner_count, dtype=jnp.int32)[None, :]).astype(
        jnp.int32
    )
    before = jnp.cumsum(hits, axis=0) - hits
    return jnp.sum(before * hits, axis=1)


def local(
    tokens,
    segment_ids,
    routes,
    owners,
    gain_attn,
    w_query,
    w_kv,
    w_out,
    gain_moe,
    w_router,
    w_gate,
    w_up,
    w_down,
):
    seq_count = lax.axis_size("seq")
    ten_count = lax.axis_size("tensor")
    seq_rank = lax.axis_index("seq")
    ten_rank = lax.axis_index("tensor")
    rows, width = tokens.shape
    total = segment_ids.shape[0]
    kv_local = w_kv.shape[1] // (2 * HEAD_DIM)
    kv_width = 2 * kv_local * HEAD_DIM
    group = HEADS // KV_HEADS
    seg_all, owner_all = segment_layout(segment_ids, owners)
    slot_all = owner_slots(owner_all, seq_count)
    first = seq_rank * rows
    seg_start = lax.dynamic_slice_in_dim(seg_all, first, rows)
    owner_tok = lax.dynamic_slice_in_dim(owner_all, first, rows)
    slot_tok = lax.dynamic_slice_in_dim(slot_all, first, rows)
    token_index = first + jnp.arange(rows, dtype=jnp.int32)
    position = token_index - seg_start
    normed = rms_norm(tokens, gain_attn)
    queries = jnp.dot(normed, w_query, preferred_element_type=jnp.float32).reshape(
        rows, kv_local * group, HEAD_DIM
    )
    queries = rotate(queries, position).astype(jnp.bfloat16)
    pairs = jnp.dot(normed, w_kv, preferred_element_type=jnp.float32).reshape(
        rows, kv_local, 2, HEAD_DIM
    )
    keys = rotate(pairs[:, :, 0], position).astype(jnp.bfloat16)
    values = pairs[:, :, 1].astype(jnp.bfloat16)
    grouped = queries.reshape(rows, kv_local, group, HEAD_DIM)
    scale = HEAD_DIM ** (-0.5)
    stacked = jnp.stack(
        [keys.reshape(rows, kv_local * HEAD_DIM), values.reshape(rows, kv_local * HEAD_DIM)]
    )
    piece = lax.all_gather(stacked, "seq", axis=1, tiled=True)
    running = jnp.full((kv_local, group, rows), FLOOR, jnp.float32)
    count = piece.shape[1]
    key_piece = piece[0].reshape(count, kv_local, HEAD_DIM)
    value_piece = piece[1].reshape(count, kv_local, HEAD_DIM)
    key_index = jnp.arange(count, dtype=jnp.int32)
    allowed = (key_index[None, :] <= token_index[:, None]) & (
        key_index[None, :] >= seg_start[:, None]
    )
    scores = (
        jnp.einsum("qkgd,nkd->kgqn", grouped, key_piece, preferred_element_type=jnp.float32) * scale
    )
    scores = jnp.where(allowed[None, None], scores, FLOOR)
    new_top = jnp.maximum(running, jnp.max(scores, axis=-1))
    weights = jnp.where(allowed[None, None], jnp.exp(scores - new_top[..., None]), 0.0)
    mass = jnp.sum(weights, axis=-1)
    accum = jnp.einsum(
        "kgqn,nkd->kgqd",
        weights.astype(jnp.bfloat16),
        value_piece,
        preferred_element_type=jnp.float32,
    )
    running, mass, accum = (new_top, mass, accum)
    attended = (
        (accum / mass[..., None])
        .transpose(2, 0, 1, 3)
        .reshape(rows, kv_local * group * HEAD_DIM)
        .astype(jnp.bfloat16)
    )
    partial_value = jnp.dot(attended, w_out, preferred_element_type=jnp.float32)
    share = width // ten_count
    column = ten_rank * share
    attn_sum = lax.psum(partial_value.astype(jnp.bfloat16), "tensor").astype(jnp.float32)
    residual = (tokens.astype(jnp.float32) + attn_sum).astype(jnp.bfloat16)
    payload = rms_norm(residual, gain_moe)
    logits = jnp.dot(payload.astype(jnp.float32), w_router, preferred_element_type=jnp.float32)
    residual_share = lax.dynamic_slice_in_dim(residual, column, share, 1)
    topk = routes.shape[1]
    expert_ids = jnp.arange(EXPERTS, dtype=jnp.int32)
    picked = routes[:, :, None] == expert_ids[None, None, :]
    chosen = jnp.sum(jnp.where(picked, logits[:, None, :], 0.0), axis=2)
    gates = jax.nn.softmax(chosen, axis=1)
    capacity = rows // 2
    holders = seq_count // EXPERTS
    flat_routes = routes.reshape(-1)
    hits = (flat_routes[:, None] == expert_ids[None, :]).astype(jnp.int32)
    ranks = jnp.sum((jnp.cumsum(hits, axis=0) - hits) * hits, axis=1)
    places = flat_routes * capacity + ranks
    sources = (
        jnp.full((EXPERTS * capacity,), rows, jnp.int32)
        .at[places]
        .set(jnp.arange(rows * topk, dtype=jnp.int32) // topk)
    )
    padded = jnp.concatenate([payload, jnp.zeros((1, payload.shape[1]), jnp.bfloat16)], axis=0)
    outgoing = padded[sources].reshape(EXPERTS, 1, capacity, payload.shape[1])
    outgoing = jnp.broadcast_to(outgoing, (EXPERTS, holders, capacity, payload.shape[1])).reshape(
        seq_count, capacity, payload.shape[1]
    )
    received = lax.all_to_all(outgoing, "seq", split_axis=0, concat_axis=0, tiled=True)
    senders, count, columns = received.shape
    flat = received.reshape(senders * count, columns)
    gate_h = jnp.dot(flat, w_gate, preferred_element_type=jnp.float32)
    up_h = jnp.dot(flat, w_up, preferred_element_type=jnp.float32)
    active = (jax.nn.silu(gate_h) * up_h).astype(jnp.bfloat16)
    block_rows = jnp.dot(active, w_down, preferred_element_type=jnp.float32)
    summed = lax.psum_scatter(
        block_rows.astype(jnp.bfloat16), "tensor", scatter_dimension=1, tiled=True
    )
    returned = lax.all_to_all(
        summed.reshape(senders, count, summed.shape[1]),
        "seq",
        split_axis=0,
        concat_axis=0,
        tiled=True,
    )
    merged = jnp.sum(
        returned.astype(jnp.float32).reshape(EXPERTS, holders, capacity, share), axis=1
    ).reshape(EXPERTS * capacity, share)
    per_route = merged[places].reshape(rows, topk, share)
    mixture = jnp.sum(gates[:, :, None] * per_route, axis=1)
    layer_out = (residual_share.astype(jnp.float32) + mixture).astype(jnp.bfloat16)
    kv_rows = jnp.stack([keys, values], axis=2).reshape(rows, kv_width)
    targets = jnp.arange(seq_count, dtype=jnp.int32)
    mine = owner_tok[None, :] == targets[:, None]
    send_rows = jnp.where(mine[:, :, None], kv_rows[None], jnp.zeros((), jnp.bfloat16))
    send_slots = jnp.where(mine, slot_tok[None, :], total)
    got_rows, got_slots = (
        lax.all_to_all(send_rows, "seq", split_axis=0, concat_axis=0, tiled=True),
        lax.all_to_all(send_slots, "seq", split_axis=0, concat_axis=0, tiled=True),
    )
    kv_cache = (
        jnp.zeros((total + 1, kv_width), jnp.bfloat16)
        .at[got_slots.reshape(-1)]
        .set(got_rows.reshape(-1, kv_width))[:total]
    )
    return (layer_out, kv_cache)


def solution(mesh):
    return jax.shard_map(
        local,
        mesh=mesh,
        in_specs=(
            P("seq", None),
            P(),
            P("seq", None),
            P(),
            P(),
            P(None, "tensor"),
            P(None, "tensor"),
            P("tensor", None),
            P(),
            P(),
            P(None, ("seq", "tensor")),
            P(None, ("seq", "tensor")),
            P(("seq", "tensor"), None),
        ),
        out_specs=(P("seq", "tensor"), P("seq", "tensor")),
        check_vma=False,
    )
```

profile of v0, /device:TPU:0, one launch (start us, length us, event | category | flops | bytes accessed | tf_op | source)
XLA Modules:
  0.0 315.2 jit_solution(11753839603998363189)
XLA Ops:
  7.3 1.5 fusion.6
  8.8 3.4 %fusion.26 = f32[128,512]{1,0:T(8,128)S(1)} fusion(bf16[4096,512]{1,0:T(8,128)(2,1)} %param.19, bf16[128,4096]{1,0:T(8,128)(2,1)} %param.13, f32[4096]{0:T(1024)} %param.17, f32[128]{0:T(128)S(1)} %add_rsqrt_fusion.1), kind=kOutput, calls=%fused_computation.41 | convolution fusion | flops 538968064 | bytes 5521920 | tf_op jit(solution)/shard_map/dot_general | solution.py:93
  12.2 0.2 reshape.439
  12.4 0.1 slice.56
  12.5 0.1 slice.59
  12.6 0.1 convert_reduce_fusion
  12.9 0.1 reduce
  13.0 0.1 copy.78
  13.1 0.1 copy.79
  13.3 0.1 select_reduce_fusion
  13.5 0.2 multiply_cosine_fusion
  13.8 0.7 pad_maximum_fusion
  14.5 0.1 copy.60
  14.6 0.1 copy.61
  14.7 4.7 %convolution_bitcast_fusion = f32[16,8,8,128]{3,1,2,0:T(8,128)S(1)} fusion(bf16[4096,1024]{1,0:T(8,128)(2,1)} %param.18, bf16[128,4096]{1,0:T(8,128)(2,1)S(1)} %copy-done.1, f32[4096]{0:T(1024)S(1)} %copy-done.3, f32[128]{0:T(128)S(1)} %add_rsqrt_fusion.1), kind=kOutput, calls=%fused_computation.27 | convolution fusion | flops 1075838976 | bytes 9978368 | tf_op jit(solution)/shard_map/dot_general | solution.py:89
  19.4 0.1 copy.80
  19.5 0.3 subtract_convert_fusion
  19.9 0.1 copy.68
  20.0 0.1 eq.114
  20.2 0.6 reduce-window.24
  20.8 0.1 fusion.24
  20.9 20.0 %all-gather.2.cloned.1.call-done = bf16[2,1024,256]{1,2,0:T(8,128)(2,1)} async-done(((bf16[2,128,256]{1,2,0:T(8,128)(2,1)}), bf16[2,1024,256]{1,2,0:T(8,128)(2,1)}) %all-gather.2.cloned.1.call-update) | async-done | bytes 1048592 | tf_op jit(solution)/shard_map/all_gather | solution.py:103
  40.9 1.3 fusion.49
  42.2 1.0 fusion
  43.2 1.0 fusion.1
  44.2 1.2 fusion.19
  45.4 1.0 slice-done.1
  46.4 2.3 convolution_convert_fusion.1
  48.8 0.2 slice_reduce_fusion.1
  49.0 0.1 eq.110
  49.2 0.1 copy.67
  49.3 0.1 mul.215
  49.4 0.1 fusion.37
  49.5 1.4 scatter_custom_fusion
  50.9 49.7 %all-reduce.3.cloned.1.call-done = bf16[128,4096]{1,0:T(8,128)(2,1)} async-done(((bf16[128,4096]{1,0:T(8,128)(2,1)}), bf16[128,4096]{1,0:T(8,128)(2,1)}) %all-reduce.3.cloned.1.call-update) | async-done | bytes 1048592 | tf_op jit(solution)/shard_map/psum | solution.py:135
  100.7 1.7 fusion.3
  102.4 0.3 fusion.5
  102.7 0.1 concatenate.37
  102.8 4.4 %gather_fusion = bf16[512,4096]{1,0:T(8,128)(2,1)} fusion(bf16[129,4096]{1,0:T(8,128)(2,1)S(1)} %concatenate.37, s32[1024]{0:T(1024)S(1)} %pad_clamp_fusion.1), kind=kCustom, calls=%fused_computation | custom fusion | bytes 8390656 | tf_op jit(solution)/shard_map/gather | solution.py:157
  107.2 53.5 %all_to_all.21 = bf16[8,64,4096]{2,1,0:T(8,128)(2,1)} all-to-all(bf16[8,64,4096]{2,1,0:T(8,128)(2,1)} %bitcast.104), channel_id=1, replica_groups=mesh['seq'=8,'tensor'=4] {'seq'}, dimensions={0} | all-to-all | bytes 8388608 | tf_op jit(solution)/shard_map/all_to_all | solution.py:161
  160.8 14.9 %fusion.51 = f32[512,2048]{1,0:T(8,128)} fusion(bf16[512,4096]{1,0:T(8,128)(2,1)} %bitcast.20, bf16[4096,2048]{1,0:T(8,128)(2,1)} %param.23), kind=kOutput, calls=%fused_computation.107 | convolution fusion | flops 8589934592 | bytes 25165824 | tf_op jit(solution)/shard_map/dot_general | solution.py:164
  175.7 31.3 %convolution_convert_fusion = bf16[512,4096]{1,0:T(8,128)(2,1)} fusion(bf16[2048,4096]{1,0:T(8,128)(2,1)} %param.25, f32[512,2048]{1,0:T(8,128)} %fusion.51, bf16[512,4096]{1,0:T(8,128)(2,1)} %bitcast.20, bf16[4096,2048]{1,0:T(8,128)(2,1)} %param.24), kind=kOutput, calls=%fused_computation.4 | convolution fusion | flops 17188257792 | bytes 46137344 | tf_op jit(solution)/shard_map/dot_general | solution.py:167
  207.1 2.3 reduce-window.31
  209.3 0.3 slice_reduce_fusion
  209.6 0.2 reduce-window.32
  210.0 0.6 compare_select_fusion.1
  210.6 3.3 %all-to-all-start.2 = ((s32[8,1,128]{2,1,0:T(1,128)}), s32[8,1,128]{2,1,0:T(1,128)S(1)}, u32[]{:S(2)}, u32[]{:S(2)}) async-start(s32[8,1,128]{2,1,0:T(1,128)} %compare_select_fusion.1), calls=%async_computation.3 | async-start | bytes 8192 | tf_op jit(solution)/shard_map/all_to_all | solution.py:191
  213.9 0.1 copy.72
  214.1 1.2 broadcast_select_fusion
  215.2 3.2 %all-to-all-done.2 = s32[8,1,128]{2,1,0:T(1,128)S(1)} async-done(((s32[8,1,128]{2,1,0:T(1,128)}), s32[8,1,128]{2,1,0:T(1,128)S(1)}, u32[]{:S(2)}, u32[]{:S(2)}) %all-to-all-start.2) | async-done | bytes 4128 | tf_op jit(solution)/shard_map/all_to_all | solution.py:191
  218.4 3.6 %all-to-all-start.3 = ((bf16[8,128,512]{2,1,0:T(8,128)(2,1)}), bf16[8,128,512]{2,1,0:T(8,128)(2,1)S(1)}, u32[]{:S(2)}, u32[]{:S(2)}) async-start(bf16[8,128,512]{2,1,0:T(8,128)(2,1)} %broadcast_select_fusion), calls=%async_computation.4 | async-start | bytes 2097152 | tf_op jit(solution)/shard_map/all_to_all | solution.py:190
  222.0 15.3 %all-to-all-done.3 = bf16[8,128,512]{2,1,0:T(8,128)(2,1)S(1)} async-done(((bf16[8,128,512]{2,1,0:T(8,128)(2,1)}), bf16[8,128,512]{2,1,0:T(8,128)(2,1)S(1)}, u32[]{:S(2)}, u32[]{:S(2)}) %all-to-all-start.3) | async-done | bytes 1048608 | tf_op jit(solution)/shard_map/all_to_all | solution.py:190
  237.3 44.2 %reduce-scatter.2.cloned.1.call-done = bf16[512,1024]{1,0:T(8,128)(2,1)} async-done(((bf16[512,4096]{1,0:T(8,128)(2,1)}), bf16[512,1024]{1,0:T(8,128)(2,1)}) %reduce-scatter.2.cloned.1.call-update) | async-done | bytes 1048592 | tf_op jit(solution)/shard_map/reduce_scatter | solution.py:168
  281.5 4.5 %all-to-all-start.1 = ((bf16[8,64,1024]{2,1,0:T(8,128)(2,1)}), bf16[8,64,1024]{2,1,0:T(8,128)(2,1)}, u32[]{:S(2)}, u32[]{:S(2)}) async-start(bf16[8,64,1024]{2,1,0:T(8,128)(2,1)} %bitcast.109), calls=%async_computation.2 | async-start | bytes 2097152 | tf_op jit(solution)/shard_map/all_to_all | solution.py:171
  286.0 5.8 %scatter_custom_fusion.1 = bf16[1025,512]{1,0:T(8,128)(2,1)S(1)} fusion(s32[1024]{0:T(1024)S(1)} %bitcast.123, bf16[1024,512]{1,0:T(8,128)(2,1)} %bitcast.110, bf16[]{:T(256)} %constant.80.clone.1), kind=kCustom, calls=%fused_computation.33 | custom fusion | bytes 1050112 | tf_op jit(solution)/shard_map/scatter | solution.py:196
  291.8 1.0 slice.66
  292.8 0.4 fusion.50
  293.3 0.1 copy.66
  293.4 7.7 %all-to-all-done.1 = bf16[8,64,1024]{2,1,0:T(8,128)(2,1)} async-done(((bf16[8,64,1024]{2,1,0:T(8,128)(2,1)}), bf16[8,64,1024]{2,1,0:T(8,128)(2,1)}, u32[]{:S(2)}, u32[]{:S(2)}) %all-to-all-start.1) | async-done | bytes 1048608 | tf_op jit(solution)/shard_map/all_to_all | solution.py:171
  301.2 1.5 bitcast_convert_fusion
  302.6 2.0 gather_fusion.1
  304.7 1.8 reshape.446
  306.5 1.3 multiply_reduce_fusion
  307.9 0.8 add_convert_fusion
  (63 shorter events, 1.1 us)
Async XLA Ops:
  7.2 285.7 %copy-start = (f32[4096,8]{0,1:T(8,128)S(1)}, f32[4096,8]{0,1:T(8,128)}, u32[]{:S(2)}) copy-start(f32[4096,8]{0,1:T(8,128)} %param.22) | copy-start | bytes 393220
  7.2 5.4 %copy-start.6 = (s32[1024]{0:T(1024)S(1)}, s32[1024]{0:T(1024)}, u32[]{:S(2)}) copy-start(s32[1024]{0:T(1024)} %param.14) | copy-start | bytes 12292
  7.2 6.1 %copy-start.7 = (s32[15]{0:T(128)S(1)}, s32[15]{0:T(128)}, u32[]{:S(2)}) copy-start(s32[15]{0:T(128)} %param.16) | copy-start | bytes 184
  7.2 33.7 %all-gather.2.cloned.1.call-start = ((), (), s32[]{:S(2)}) async-start(), calls=%async_computation.5 | async-start | bytes 1179648 | tf_op jit(solution)/shard_map/all_gather | solution.py:103
  8.8 5.9 %copy-start.1 = (bf16[128,4096]{1,0:T(8,128)(2,1)S(1)}, bf16[128,4096]{1,0:T(8,128)(2,1)}, u32[]{:S(2)}) copy-start(bf16[128,4096]{1,0:T(8,128)(2,1)} %param.13) | copy-start | bytes 3145732
  8.8 5.9 %copy-start.3 = (f32[4096]{0:T(1024)S(1)}, f32[4096]{0:T(1024)}, u32[]{:S(2)}) copy-start(f32[4096]{0:T(1024)} %param.17) | copy-start | bytes 49156
  14.5 86.2 %all-reduce.3.cloned.1.call-start = ((), (), s32[]{:S(2)}) async-start(), calls=%async_computation.6 | async-start | bytes 2097152 | tf_op jit(solution)/shard_map/psum | solution.py:135
  14.7 5.2 %copy-start.5 = (s32[128,2]{0,1:T(2,128)S(1)}, s32[128,2]{0,1:T(2,128)}, u32[]{:S(2)}) copy-start(s32[128,2]{0,1:T(2,128)} %param.15) | copy-start | bytes 3076
  42.2 3.2 %slice-start = ((s8[8388608]{0:T(1024)(128)(4,1)}), s8[4194304]{0:T(1024)(128)(4,1)S(1)}, s32[]{:S(2)}) async-start(s8[8388608]{0:T(1024)(128)(4,1)} %bitcast.102), calls=%async_computation.8 | async-start | bytes 8388608
  44.2 2.2 slice-start.1
  48.7 53.7 %copy-start.4 = (f32[4096]{0:T(1024)S(1)}, f32[4096]{0:T(1024)}, u32[]{:S(2)}) copy-start(f32[4096]{0:T(1024)} %param.21) | copy-start | bytes 49156
  48.7 232.8 %reduce-scatter.2.cloned.1.call-start = ((), (), s32[]{:S(2)}) async-start(), calls=%async_computation.7 | async-start | bytes 5242880 | tf_op jit(solution)/shard_map/reduce_scatter | solution.py:168
  210.6 7.8 %all-to-all-start.2 = ((s32[8,1,128]{2,1,0:T(1,128)}), s32[8,1,128]{2,1,0:T(1,128)S(1)}, u32[]{:S(2)}, u32[]{:S(2)}) async-start(s32[8,1,128]{2,1,0:T(1,128)} %compare_select_fusion.1), calls=%async_computation.3 | async-start | bytes 8192 | tf_op jit(solution)/shard_map/all_to_all | solution.py:191
  218.4 18.9 %all-to-all-start.3 = ((bf16[8,128,512]{2,1,0:T(8,128)(2,1)}), bf16[8,128,512]{2,1,0:T(8,128)(2,1)S(1)}, u32[]{:S(2)}, u32[]{:S(2)}) async-start(bf16[8,128,512]{2,1,0:T(8,128)(2,1)} %broadcast_select_fusion), calls=%async_computation.4 | async-start | bytes 2097152 | tf_op jit(solution)/shard_map/all_to_all | solution.py:190
  237.3 48.7 %copy-start.2 = (bf16[8,128,512]{2,1,0:T(8,128)(2,1)}, bf16[8,128,512]{2,1,0:T(8,128)(2,1)S(1)}, u32[]{:S(2)}) copy-start(bf16[8,128,512]{2,1,0:T(8,128)(2,1)S(1)} %all-to-all-done.3) | copy-start | bytes 3145732
  281.5 19.7 %all-to-all-start.1 = ((bf16[8,64,1024]{2,1,0:T(8,128)(2,1)}), bf16[8,64,1024]{2,1,0:T(8,128)(2,1)}, u32[]{:S(2)}, u32[]{:S(2)}) async-start(bf16[8,64,1024]{2,1,0:T(8,128)(2,1)} %bitcast.109), calls=%async_computation.2 | async-start | bytes 2097152 | tf_op jit(solution)/shard_map/all_to_all | solution.py:171
Sparse Core Ops, SparseCore 0:
  14.6 26.2 all-gather.1
  48.8 51.8 all-reduce.2
  207.1 74.3 reduce-scatter.1
where the time goes:
time: 316 us; the launch traced here: 315 us
  waiting for transfers between devices  140 us (44%)
  matrix products  59 us (19%)
  blocking collectives  53.5 us (17%)
  local copies, waits for them, and re-layouts  21.6 us (7%)
  other arithmetic  15.1 us (5%)
  between operations  14.3 us (5%)
  starting transfers between devices  11.4 us (4%)
    all_to_all x1, blocking collectives, local(): lax.all_to_all(outgoing, 'seq', split_axis=0, concat_axis=0, tiled=True)  53.5 us
    psum x1, waiting for transfers between devices, local(): lax.psum(partial_value.astype(jnp.bfloat16), 'tensor').astype(jnp.float32)  49.7 us
    reduce_scatter x1, waiting for transfers between devices, local(): lax.psum_scatter(block_rows.astype(jnp.bfloat16), 'tensor', scatter_dimen...  44.2 us
    dot_general x1, matrix products, local(): block_rows = jnp.dot(active, w_down, preferred_element_type=jnp.float32)  31.3 us
    all_gather x1, waiting for transfers between devices, local(): piece = lax.all_gather(stacked, 'seq', axis=1, tiled=True)  20 us
    all_to_all x1, waiting for transfers between devices, local(): lax.all_to_all(send_rows, 'seq', split_axis=0, concat_axis=0, tiled=True)  15.3 us
    dot_general x1, matrix products, local(): gate_h = jnp.dot(flat, w_gate, preferred_element_type=jnp.float32)  14.9 us
    all_to_all x1, waiting for transfers between devices, local(): lax.all_to_all(summed.reshape(senders, count, summed.shape[1]), 'seq', sp...  7.72 us
  transfers between devices with their start and end apart: 6, of which 6 were waited for; matrix products, arithmetic and copies ran while one was open for 7% of the time, Pallas kernels for 0%

commit v1 on v0

--- a/solution.py
+++ b/solution.py
@@ -33,24 +33,31 @@
     )
 
 
-def segment_layout(segment_ids, owners):
+def segment_layout(segment_ids, owners, token_index):
     short_count = owners.shape[0] - 1
     labels = jnp.where(segment_ids < 0, short_count + 1, segment_ids)
+    mine = jnp.sum(
+        jnp.where(
+            jnp.arange(segment_ids.shape[0], dtype=jnp.int32)[None, :] == token_index[:, None],
+            labels[None, :],
+            0,
+        ),
+        axis=1,
+    )
+    seg_start = jnp.sum((labels[None, :] < mine[:, None]).astype(jnp.int32), axis=1)
+    owner_ext = jnp.concatenate([owners, jnp.full((1,), -1, jnp.int32)])
     onehot = labels[:, None] == jnp.arange(short_count + 2, dtype=jnp.int32)[None, :]
-    counts = jnp.sum(onehot.astype(jnp.int32), axis=0)
-    starts = jnp.cumsum(counts) - counts
-    seg_start = jnp.sum(jnp.where(onehot, starts[None, :], 0), axis=1)
-    owner_ext = jnp.concatenate([owners, jnp.full((1,), -1, jnp.int32)])
-    owner_tok = jnp.sum(jnp.where(onehot, owner_ext[None, :], 0), axis=1)
-    return (seg_start, owner_tok)
-
-
-def owner_slots(owner_tok, owner_count):
-    hits = (owner_tok[:, None] == jnp.arange(owner_count, dtype=jnp.int32)[None, :]).astype(
-        jnp.int32
-    )
-    before = jnp.cumsum(hits, axis=0) - hits
-    return jnp.sum(before * hits, axis=1)
+    owner_all = jnp.sum(jnp.where(onehot, owner_ext[None, :], 0), axis=1)
+    return (seg_start, owner_all)
+
+
+def cache_places(owner_all, owner):
+    total = owner_all.shape[0]
+    index = jnp.arange(total, dtype=jnp.int32)
+    mine = owner_all == owner
+    slots = jnp.sum(((index[None, :] < index[:, None]) & mine[None, :]).astype(jnp.int32), axis=1)
+    slots = jnp.where(mine, slots, total)
+    return (index[:, None] == slots[None, :]).astype(jnp.bfloat16)
 
 
 def local(
@@ -73,17 +80,12 @@
     seq_rank = lax.axis_index("seq")
     ten_rank = lax.axis_index("tensor")
     rows, width = tokens.shape
-    total = segment_ids.shape[0]
     kv_local = w_kv.shape[1] // (2 * HEAD_DIM)
     kv_width = 2 * kv_local * HEAD_DIM
     group = HEADS // KV_HEADS
-    seg_all, owner_all = segment_layout(segment_ids, owners)
-    slot_all = owner_slots(owner_all, seq_count)
     first = seq_rank * rows
-    seg_start = lax.dynamic_slice_in_dim(seg_all, first, rows)
-    owner_tok = lax.dynamic_slice_in_dim(owner_all, first, rows)
-    slot_tok = lax.dynamic_slice_in_dim(slot_all, first, rows)
     token_index = first + jnp.arange(rows, dtype=jnp.int32)
+    seg_start, owner_all = segment_layout(segment_ids, owners, token_index)
     position = token_index - seg_start
     normed = rms_norm(tokens, gain_attn)
     queries = jnp.dot(normed, w_query, preferred_element_type=jnp.float32).reshape(
@@ -97,14 +99,16 @@
     values = pairs[:, :, 1].astype(jnp.bfloat16)
     grouped = queries.reshape(rows, kv_local, group, HEAD_DIM)
     scale = HEAD_DIM ** (-0.5)
-    stacked = jnp.stack(
-        [keys.reshape(rows, kv_local * HEAD_DIM), values.reshape(rows, kv_local * HEAD_DIM)]
-    )
-    piece = lax.all_gather(stacked, "seq", axis=1, tiled=True)
+    kv_rows = jnp.stack([keys, values], axis=2).reshape(rows, kv_width)
+    piece = lax.all_gather(kv_rows, "seq", axis=0, tiled=True)
+    kv_cache = jnp.dot(
+        cache_places(owner_all, seq_rank), piece, preferred_element_type=jnp.float32
+    ).astype(jnp.bfloat16)
     running = jnp.full((kv_local, group, rows), FLOOR, jnp.float32)
-    count = piece.shape[1]
-    key_piece = piece[0].reshape(count, kv_local, HEAD_DIM)
-    value_piece = piece[1].reshape(count, kv_local, HEAD_DIM)
+    count = piece.shape[0]
+    pieces = piece.reshape(count, kv_local, 2, HEAD_DIM)
+    key_piece = pieces[:, :, 0]
+    value_piece = pieces[:, :, 1]
     key_index = jnp.arange(count, dtype=jnp.int32)
     allowed = (key_index[None, :] <= token_index[:, None]) & (
         key_index[None, :] >= seg_start[:, None]
@@ -144,17 +148,22 @@
     gates = jax.nn.softmax(chosen, axis=1)
     capacity = rows // 2
     holders = seq_count // EXPERTS
-    flat_routes = routes.reshape(-1)
-    hits = (flat_routes[:, None] == expert_ids[None, :]).astype(jnp.int32)
-    ranks = jnp.sum((jnp.cumsum(hits, axis=0) - hits) * hits, axis=1)
-    places = flat_routes * capacity + ranks
-    sources = (
-        jnp.full((EXPERTS * capacity,), rows, jnp.int32)
-        .at[places]
-        .set(jnp.arange(rows * topk, dtype=jnp.int32) // topk)
-    )
-    padded = jnp.concatenate([payload, jnp.zeros((1, payload.shape[1]), jnp.bfloat16)], axis=0)
-    outgoing = padded[sources].reshape(EXPERTS, 1, capacity, payload.shape[1])
+    hits = jnp.any(picked, axis=1)
+    row_index = jnp.arange(rows, dtype=jnp.int32)
+    earlier = (row_index[None, :] < row_index[:, None]).astype(jnp.bfloat16)
+    before = jnp.dot(
+        earlier, hits.astype(jnp.bfloat16), preferred_element_type=jnp.float32
+    ).astype(jnp.int32)
+    slot_of = jnp.where(hits, before, -1)
+    slot_index = jnp.arange(capacity, dtype=jnp.int32)
+    sources = (slot_of.T[:, None, :] == slot_index[None, :, None]).astype(jnp.bfloat16)
+    outgoing = (
+        jnp.dot(
+            sources.reshape(EXPERTS * capacity, rows), payload, preferred_element_type=jnp.float32
+        )
+        .astype(jnp.bfloat16)
+        .reshape(EXPERTS, 1, capacity, payload.shape[1])
+    )
     outgoing = jnp.broadcast_to(outgoing, (EXPERTS, holders, capacity, payload.shape[1])).reshape(
         seq_count, capacity, payload.shape[1]
     )
@@ -175,26 +184,21 @@
         concat_axis=0,
         tiled=True,
     )
-    merged = jnp.sum(
-        returned.astype(jnp.float32).reshape(EXPERTS, holders, capacity, share), axis=1
-    ).reshape(EXPERTS * capacity, share)
-    per_route = merged[places].reshape(rows, topk, share)
-    mixture = jnp.sum(gates[:, :, None] * per_route, axis=1)
+    rank_of = jnp.sum(jnp.where(picked, before[:, None, :], 0), axis=2)
+    place_of = routes * capacity + rank_of
+    slots = jnp.arange(EXPERTS * capacity, dtype=jnp.int32)
+    takes = (place_of.T[:, :, None] == slots[None, None, :]).astype(jnp.bfloat16)
+    takes = jnp.broadcast_to(
+        takes.reshape(topk, rows, EXPERTS, 1, capacity),
+        (topk, rows, EXPERTS, holders, capacity),
+    ).reshape(topk * rows, seq_count * capacity)
+    per_route = jnp.dot(
+        takes,
+        returned.reshape(seq_count * capacity, share),
+        preferred_element_type=jnp.float32,
+    ).reshape(topk, rows, share)
+    mixture = jnp.sum(gates.T[:, :, None] * per_route, axis=0)
     layer_out = (residual_share.astype(jnp.float32) + mixture).astype(jnp.bfloat16)
-    kv_rows = jnp.stack([keys, values], axis=2).reshape(rows, kv_width)
-    targets = jnp.arange(seq_count, dtype=jnp.int32)
-    mine = owner_tok[None, :] == targets[:, None]
-    send_rows = jnp.where(mine[:, :, None], kv_rows[None], jnp.zeros((), jnp.bfloat16))
-    send_slots = jnp.where(mine, slot_tok[None, :], total)
-    got_rows, got_slots = (
-        lax.all_to_all(send_rows, "seq", split_axis=0, concat_axis=0, tiled=True),
-        lax.all_to_all(send_slots, "seq", split_axis=0, concat_axis=0, tiled=True),
-    )
-    kv_cache = (
-        jnp.zeros((total + 1, kv_width), jnp.bfloat16)
-        .at[got_slots.reshape(-1)]
-        .set(got_rows.reshape(-1, kv_width))[:total]
-    )
     return (layer_out, kv_cache)
 
 

time: 316 us -> 305 us (0.965)
  waiting for transfers between devices: 140 us -> 159 us
  local copies, waits for them, and re-layouts: 21.6 us -> 4.69 us
  other arithmetic: 15.1 us -> 7.39 us
  starting transfers between devices: 11.4 us -> 3.78 us
  matrix products: 59 us -> 63.4 us
    reduce_scatter x1, waiting for transfers between devices: 44.2 us -> 73.4 us  [local(): lax.psum_scatter(block_rows.astype(jnp.bfloat16), 'tensor', scatter_dimen...]
    all_to_all x2 -> x0, waiting for transfers between devices: 18.5 us -> none  [the longest x1 15.3 us: local(): lax.all_to_all(send_rows, 'seq', split_axis=0, concat_axis=0, tiled=True)]
    scatter x2 -> x0, local copies, waits for them, and re-layouts: 7.21 us -> none  [the longest x1 5.82 us: local(): kv_cache = jnp.zeros((total + 1, kv_width), jnp.bfloat16).at[got_slots.re...]
    all_to_all x2 -> x0, starting transfers between devices: 6.87 us -> none  [the longest x1 3.56 us: local(): lax.all_to_all(send_rows, 'seq', split_axis=0, concat_axis=0, tiled=True)]
    gather x2 -> x0, local copies, waits for them, and re-layouts: 6.44 us -> none  [the longest x1 4.4 us: local(): outgoing = padded[sources].reshape(EXPERTS, 1, capacity, payload.shape[1])]
    all_to_all x1, waiting for transfers between devices: 7.72 us -> 12.6 us  [local(): lax.all_to_all(summed.reshape(senders, count, summed.shape[1]), 'seq', sp...]
    dot_general x0 -> x4, matrix products: none -> 4.22 us  [the longest x1 2.26 us: local(): jnp.dot(cache_places(owner_all, seq_rank), piece, preferred_element_type=...]
    another operation x9 -> x1, other arithmetic: 4.15 us -> 0.27 us
  transfers between devices with their start and end apart: 6 -> 4, of which waited for: 6 -> 4; matrix products, arithmetic and copies ran while one was open for 7% -> 3% of each run, Pallas kernels for 0% -> 0%
where the time goes in v1:
time: 305 us; the launch traced here: 304 us
  waiting for transfers between devices  159 us (52%)
  matrix products  63.4 us (21%)
  blocking collectives  52.5 us (17%)
  between operations  14.1 us (5%)
  other arithmetic  7.39 us (2%)
  local copies, waits for them, and re-layouts  4.69 us (2%)
  starting transfers between devices  3.78 us (1%)
    reduce_scatter x1, waiting for transfers between devices, local(): lax.psum_scatter(block_rows.astype(jnp.bfloat16), 'tensor', scatter_dimen...  73.4 us
    all_to_all x1, blocking collectives, local(): lax.all_to_all(outgoing, 'seq', split_axis=0, concat_axis=0, tiled=True)  52.5 us
    psum x1, waiting for transfers between devices, local(): lax.psum(partial_value.astype(jnp.bfloat16), 'tensor').astype(jnp.float32)  51.5 us
    dot_general x1, matrix products, local(): block_rows = jnp.dot(active, w_down, preferred_element_type=jnp.float32)  31.2 us
    all_gather x1, waiting for transfers between devices, local(): piece = lax.all_gather(kv_rows, 'seq', axis=0, tiled=True)  20.9 us
    dot_general x1, matrix products, local(): gate_h = jnp.dot(flat, w_gate, preferred_element_type=jnp.float32)  13.9 us
    all_to_all x1, waiting for transfers between devices, local(): lax.all_to_all(summed.reshape(senders, count, summed.shape[1]), 'seq', sp...  12.6 us
  transfers between devices with their start and end apart: 4, of which 4 were waited for; matrix products, arithmetic and copies ran while one was open for 3% of the time, Pallas kernels for 0%

profile of v1, /device:TPU:0, one launch (start us, length us, event | category | flops | bytes accessed | tf_op | source)
XLA Modules:
  0.0 304.4 jit_solution(17777325623967351373)
XLA Ops:
  7.2 0.0 copy-start
  7.2 0.0 copy-start.7
  7.2 0.0 all-gather.2.cloned.1.call-start
  7.3 1.5 fusion.8
  8.8 0.0 copy-start.4
  8.8 3.4 %fusion.32 = f32[128,512]{1,0:T(8,128)S(1)} fusion(bf16[4096,512]{1,0:T(8,128)(2,1)} %param.19, bf16[128,4096]{1,0:T(8,128)(2,1)} %param.13, f32[4096]{0:T(1024)} %param.17, f32[128]{0:T(128)S(1)} %add_rsqrt_fusion.1), kind=kOutput, calls=%fused_computation.51 | convolution fusion | flops 538968064 | bytes 5521920 | tf_op jit(solution)/shard_map/dot_general | solution.py:95
  12.2 0.2 reshape.237
  12.3 0.1 slice.36
  12.5 0.1 slice.33
  12.6 0.0 copy-done.7
  12.6 0.2 select_reduce_fusion
  12.8 0.2 convert_reduce_fusion.1
  13.1 0.1 copy.51
  13.2 0.1 copy.48
  13.3 0.2 multiply_cosine_fusion
  13.6 0.7 pad_maximum_fusion
  14.2 0.0 all-gather.2.cloned.1.call-update
  14.2 0.0 all-reduce.2.cloned.1.call-start
  14.3 0.1 copy.39
  14.4 0.1 copy.40
  14.5 0.0 copy-done.1
  14.5 0.0 copy-done.4
  14.5 4.7 %convolution_bitcast_fusion = f32[16,8,8,128]{3,1,2,0:T(8,128)S(1)} fusion(bf16[4096,1024]{1,0:T(8,128)(2,1)} %param.18, bf16[128,4096]{1,0:T(8,128)(2,1)S(1)} %copy-done.1, f32[4096]{0:T(1024)S(1)} %copy-done.4, f32[128]{0:T(128)S(1)} %add_rsqrt_fusion.1), kind=kOutput, calls=%fused_computation.33 | convolution fusion | flops 1075838976 | bytes 9978368 | tf_op jit(solution)/shard_map/dot_general | solution.py:91
  19.2 0.1 copy.52
  19.3 0.3 subtract_convert_fusion
  19.7 0.1 fusion.28
  19.8 20.9 %all-gather.2.cloned.1.call-done = bf16[1024,512]{0,1:T(8,128)(2,1)} async-done(((bf16[128,512]{0,1:T(8,128)(2,1)}), bf16[1024,512]{0,1:T(8,128)(2,1)}) %all-gather.2.cloned.1.call-update) | async-done | bytes 1048592 | tf_op jit(solution)/shard_map/all_gather | solution.py:103
  40.7 0.0 copy-start.3
  40.7 0.0 slice-start
  40.7 2.2 fusion.2
  42.9 1.0 fusion.3
  43.9 0.0 copy-done.3
  43.9 0.0 slice-start.1
  43.9 1.2 fusion.24
  45.1 0.0 slice-done
  45.1 1.0 slice-done.1
  46.1 2.3 convolution_convert_fusion.2
  48.3 0.0 all-reduce.2.cloned.1.call-update
  48.4 0.0 reduce-scatter.2.cloned.1.call-start
  48.4 0.1 eq.124
  48.5 0.0 copy-done.6
  48.5 0.1 convolution_convert_fusion.3
  48.7 0.2 bitcast_compare_fusion
  48.8 51.5 %all-reduce.2.cloned.1.call-done = bf16[128,4096]{1,0:T(8,128)(2,1)} async-done(((bf16[128,4096]{1,0:T(8,128)(2,1)}), bf16[128,4096]{1,0:T(8,128)(2,1)}) %all-reduce.2.cloned.1.call-update) | async-done | bytes 1048592 | tf_op jit(solution)/shard_map/psum | solution.py:139
  100.4 1.7 fusion.5
  102.1 0.0 copy-done.5
  102.1 1.3 convolution_convert_fusion.1
  103.4 52.5 %all_to_all.10 = bf16[8,64,4096]{2,1,0:T(8,128)(2,1)S(1)} all-to-all(bf16[8,64,4096]{2,1,0:T(8,128)(2,1)S(1)} %bitcast.85), channel_id=1, replica_groups=mesh['seq'=8,'tensor'=4] {'seq'}, dimensions={0} | all-to-all | bytes 8388608 | tf_op jit(solution)/shard_map/all_to_all | solution.py:170
  155.9 2.0 copy-done.2
  157.9 13.9 %fusion.51 = f32[512,2048]{1,0:T(8,128)} fusion(bf16[512,4096]{1,0:T(8,128)(2,1)S(1)} %bitcast.89, bf16[4096,2048]{1,0:T(8,128)(2,1)} %param.23), kind=kOutput, calls=%fused_computation.92 | convolution fusion | flops 8589934592 | bytes 25165824 | tf_op jit(solution)/shard_map/dot_general | solution.py:173
  171.8 31.2 %convolution_convert_fusion = bf16[512,4096]{1,0:T(8,128)(2,1)} fusion(bf16[2048,4096]{1,0:T(8,128)(2,1)} %param.25, f32[512,2048]{1,0:T(8,128)} %fusion.51, bf16[512,4096]{1,0:T(8,128)(2,1)} %bitcast.90, bf16[4096,2048]{1,0:T(8,128)(2,1)} %param.24), kind=kOutput, calls=%fused_computation | convolution fusion | flops 17188257792 | bytes 46137344 | tf_op jit(solution)/shard_map/dot_general | solution.py:176
  203.0 0.0 reduce-scatter.2.cloned.1.call-update
  203.0 0.6 copy-done.8
  203.7 0.1 pad_add_fusion
  203.8 0.1 select_reduce_fusion.1
  203.9 0.2 convert_reduce_fusion
  204.1 73.4 %reduce-scatter.2.cloned.1.call-done = bf16[512,1024]{1,0:T(8,128)(2,1)} async-done(((bf16[512,4096]{1,0:T(8,128)(2,1)}), bf16[512,1024]{1,0:T(8,128)(2,1)}) %reduce-scatter.2.cloned.1.call-update) | async-done | bytes 1048592 | tf_op jit(solution)/shard_map/reduce_scatter | solution.py:177
  277.5 3.7 %all-to-all-start.1 = ((bf16[8,64,1024]{2,1,0:T(8,128)(2,1)}), bf16[8,64,1024]{2,1,0:T(8,128)(2,1)S(1)}, u32[]{:S(2)}, u32[]{:S(2)}) async-start(bf16[8,64,1024]{2,1,0:T(8,128)(2,1)} %bitcast.93), calls=%async_computation.2 | async-start | bytes 2097152 | tf_op jit(solution)/shard_map/all_to_all | solution.py:180
  281.2 2.3 fusion.16
  283.4 0.0 copy-done
  283.4 0.4 fusion.35
  284.0 12.6 %all-to-all-done.1 = bf16[8,64,1024]{2,1,0:T(8,128)(2,1)S(1)} async-done(((bf16[8,64,1024]{2,1,0:T(8,128)(2,1)}), bf16[8,64,1024]{2,1,0:T(8,128)(2,1)S(1)}, u32[]{:S(2)}, u32[]{:S(2)}) %all-to-all-start.1) | async-done | bytes 1048608 | tf_op jit(solution)/shard_map/all_to_all | solution.py:180
  296.6 0.5 fusion.17
  297.1 0.8 add_convert_fusion
  (27 shorter events, 0.3 us)
Async XLA Ops:
  7.2 276.3 %copy-start = (f32[4096,8]{0,1:T(8,128)S(1)}, f32[4096,8]{0,1:T(8,128)}, u32[]{:S(2)}) copy-start(f32[4096,8]{0,1:T(8,128)} %param.22) | copy-start | bytes 393220
  7.2 5.4 %copy-start.7 = (s32[1024]{0:T(1024)S(1)}, s32[1024]{0:T(1024)}, u32[]{:S(2)}) copy-start(s32[1024]{0:T(1024)} %param.14) | copy-start | bytes 12292
  7.2 33.5 %all-gather.2.cloned.1.call-start = ((), (), s32[]{:S(2)}) async-start(), calls=%async_computation.3 | async-start | bytes 1179648 | tf_op jit(solution)/shard_map/all_gather | solution.py:103
  8.8 5.7 %copy-start.1 = (bf16[128,4096]{1,0:T(8,128)(2,1)S(1)}, bf16[128,4096]{1,0:T(8,128)(2,1)}, u32[]{:S(2)}) copy-start(bf16[128,4096]{1,0:T(8,128)(2,1)} %param.13) | copy-start | bytes 3145732
  8.8 5.7 %copy-start.4 = (f32[4096]{0:T(1024)S(1)}, f32[4096]{0:T(1024)}, u32[]{:S(2)}) copy-start(f32[4096]{0:T(1024)} %param.17) | copy-start | bytes 49156
  14.2 86.1 %all-reduce.2.cloned.1.call-start = ((), (), s32[]{:S(2)}) async-start(), calls=%async_computation.4 | async-start | bytes 2097152 | tf_op jit(solution)/shard_map/psum | solution.py:139
  40.7 3.2 %copy-start.3 = (bf16[1024,512]{0,1:T(8,128)(2,1)S(1)}, bf16[1024,512]{0,1:T(8,128)(2,1)}, u32[]{:S(2)}) copy-start(bf16[1024,512]{0,1:T(8,128)(2,1)} %all-gather.2.cloned.1.call-done) | copy-start | bytes 3145732
  40.7 4.4 %slice-start = ((s8[8388608]{0:T(1024)(128)(4,1)}), s8[4194304]{0:T(1024)(128)(4,1)S(1)}, s32[]{:S(2)}) async-start(s8[8388608]{0:T(1024)(128)(4,1)} %bitcast.86), calls=%async_computation.6 | async-start | bytes 8388608
  43.9 2.2 slice-start.1
  46.1 2.4 copy-start.6
  48.3 53.7 %copy-start.5 = (f32[4096]{0:T(1024)S(1)}, f32[4096]{0:T(1024)}, u32[]{:S(2)}) copy-start(f32[4096]{0:T(1024)} %param.21) | copy-start | bytes 49156
  48.4 229.1 %reduce-scatter.2.cloned.1.call-start = ((), (), s32[]{:S(2)}) async-start(), calls=%async_computation.5 | async-start | bytes 5242880 | tf_op jit(solution)/shard_map/reduce_scatter | solution.py:177
  155.9 2.0 copy-start.2
  203.0 0.7 copy-start.8
  277.5 19.1 %all-to-all-start.1 = ((bf16[8,64,1024]{2,1,0:T(8,128)(2,1)}), bf16[8,64,1024]{2,1,0:T(8,128)(2,1)S(1)}, u32[]{:S(2)}, u32[]{:S(2)}) async-start(bf16[8,64,1024]{2,1,0:T(8,128)(2,1)} %bitcast.93), calls=%async_computation.2 | async-start | bytes 2097152 | tf_op jit(solution)/shard_map/all_to_all | solution.py:180
Sparse Core Ops, SparseCore 0:
  14.4 26.2 all-gather.1
  48.5 51.8 all-reduce.1
  203.2 74.3 reduce-scatter.1
